TPU v7x, 256 devices: a whole 4x4x8 slice. The times are simulated.
256 devices in a mesh: group: 2 (over y_lo), branch: 16 (over y_hi, x, core), tensor: 8 (over z).
Axes of the slice: x: 4, y: 4 (y_hi: 2, y_lo: 2; y = y_hi * 2 + y_lo), z: 8, core: 2. Of those that a mesh axis runs over, the one named last changes fastest.
Arguments:
- queries: bfloat16 [8192, 8192], P(('group', 'branch'), 'tensor'), parts along dimension 0, may hold values from -160 to 160
- prefix_cache: bfloat16 [2, 3072, 1024], P(None, 'group', 'tensor'), parts along dimension 1, may hold values from -5 to 5
- prior_cache: bfloat16 [2, 8192, 1024], P(None, ('group', 'branch'), 'tensor'), parts along dimension 1, may hold values from -5 to 5
- fresh_cache: bfloat16 [2, 8192, 1024], P(None, ('group', 'branch'), 'tensor'), parts along dimension 1, may hold values from -5 to 5
- visible: int32 [32, 16], P('group'), parts along dimension 0, may hold values 0 or 1
- turn_order: int32 [32], P('group'), parts along dimension 0, may hold values from 0 to 15, each once
- output_weight: bfloat16 [8192, 8192], P('tensor', 'branch'), may hold values from -0.0625 to 0.0625
Outputs:
- projected: bfloat16 [8192, 8192], P(('group', 'branch'), 'tensor'), parts along dimension 0
There are 2 independent parts, one for each index of `group`. A program takes and returns all parts, laid end to end along the dimension named above; an argument that names none is the same for every part. Nothing has to cross between parts.
Inputs may be any that keep to these rules, and one draw needn't show every extreme that they name: `turn_order`: each of 0 to 15 once.
All inputs are finite; a program needn't handle non-finite values.
Results may differ from a plain program's by a relative error of at most 0.015.
Values may be sent and summed in bfloat16 or wider, within the bound.
A program may use at most 64 MiB of HBM per device.

v0:
```python
import math

import jax
import jax.numpy as jnp
from jax import lax
from jax.sharding import PartitionSpec as P

HD = 128


NEGATIVE = -1e30


def largest_divisor(total_rows, ceiling):
    chosen = 1
    for candidate in range(1, min(total_rows, ceiling) + 1):
        if total_rows % candidate == 0:
            chosen = candidate
    return chosen


def update_state(running, query_heads, key_rows, value_rows, allowed):
    peak_old, total_old, summed_old = running
    scores = jnp.einsum(
        "qhgd,khd->hgqk", query_heads, key_rows, preferred_element_type=jnp.float32
    ) / math.sqrt(HD)
    if allowed is None:
        masked = scores
    else:
        masked = jnp.where(allowed, scores, NEGATIVE)
    peak_new = jnp.maximum(peak_old, jnp.max(masked, axis=-1))
    weights = jnp.exp(masked - peak_new[..., None])
    if allowed is not None:
        weights = jnp.where(allowed, weights, 0.0)
    factor = jnp.exp(peak_old - peak_new)
    total_new = total_old * factor + jnp.sum(weights, axis=-1)
    summed_new = summed_old * factor[..., None] + jnp.einsum(
        "hgqk,khd->hgqd",
        weights.astype(jnp.bfloat16),
        value_rows,
        preferred_element_type=jnp.float32,
    )
    return (peak_new, total_new, summed_new)


def sweep(running, query_heads, key_rows, value_rows, allow_rows):
    row_count = key_rows.shape[0]
    block_rows = largest_divisor(row_count, 1024)
    if block_rows == row_count:
        return update_state(running, query_heads, key_rows, value_rows, allow_rows(0, row_count))
    block_count = row_count // block_rows
    key_blocks = key_rows.reshape(block_count, block_rows, key_rows.shape[1], key_rows.shape[2])
    value_blocks = value_rows.reshape(
        block_count, block_rows, value_rows.shape[1], value_rows.shape[2]
    )

    def advance(state, inputs):
        key_block, value_block, position = inputs
        return (
            update_state(
                state,
                query_heads,
                key_block,
                value_block,
                allow_rows(position * block_rows, block_rows),
            ),
            None,
        )

    running, unused = lax.scan(
        advance, running, (key_blocks, value_blocks, jnp.arange(block_count, dtype=jnp.int32))
    )
    return running


def per_device(queries, prefix_cache, prior_cache, fresh_cache, visible, turn_order, output_weight):
    message_rows = queries.shape[0]
    local_heads = queries.shape[1] // HD
    local_groups = prefix_cache.shape[2] // HD
    sharing = local_heads // local_groups
    query_heads = queries.reshape(message_rows, local_groups, sharing, HD)
    agent_index = lax.axis_index("branch")
    agent_count = visible.shape[0]
    seen_row = lax.dynamic_slice_in_dim(visible, agent_index, 1, 0)[0]
    own_turn = lax.dynamic_slice_in_dim(turn_order, agent_index, 1, 0)[0]
    positions = jnp.arange(message_rows, dtype=jnp.int32)
    agent_ids = jnp.arange(agent_count, dtype=jnp.int32)

    def split_cache(cache):
        return (cache[0].reshape(-1, local_groups, HD), cache[1].reshape(-1, local_groups, HD))

    def whole_rows(offset, count):
        return None

    start_state = (
        jnp.full((local_groups, sharing, message_rows), NEGATIVE, jnp.float32),
        jnp.zeros((local_groups, sharing, message_rows), jnp.float32),
        jnp.zeros((local_groups, sharing, message_rows, HD), jnp.float32),
    )
    prefix_keys, prefix_values = split_cache(prefix_cache)
    prefix_state = sweep(start_state, query_heads, prefix_keys, prefix_values, whole_rows)

    def add_messages(running, pieces, root):
        prior_keys, prior_values = split_cache(pieces[0])
        fresh_keys, fresh_values = split_cache(pieces[1])

        def locate(offset, count):
            row_index = root + offset + jnp.arange(count, dtype=jnp.int32)
            owner_ids = row_index // message_rows
            onehot = owner_ids[:, None] == agent_ids[None, :]
            return (row_index, owner_ids, onehot)

        def prior_allowed(offset, count):
            row_index, owner_ids, onehot = locate(offset, count)
            visible_rows = jnp.sum(jnp.where(onehot, seen_row[None, :], 0), axis=1) > 0
            return visible_rows[None, :]

        def fresh_allowed(offset, count):
            row_index, owner_ids, onehot = locate(offset, count)
            turn_values = jnp.sum(jnp.where(onehot, turn_order[None, :], 0), axis=1)
            earlier = turn_values < own_turn
            causal = (owner_ids == agent_index)[None, :] & (
                (row_index % message_rows)[None, :] <= positions[:, None]
            )
            return earlier[None, :] | causal

        running = sweep(running, query_heads, prior_keys, prior_values, prior_allowed)
        return sweep(running, query_heads, fresh_keys, fresh_values, fresh_allowed)

    peak_final, total_final, summed_final = add_messages(
        prefix_state,
        (
            lax.all_gather(prior_cache, "branch", axis=1, tiled=True),
            lax.all_gather(fresh_cache, "branch", axis=1, tiled=True),
        ),
        jnp.int32(0),
    )
    heads_out = (summed_final / total_final[..., None]).astype(jnp.bfloat16)
    attention = jnp.transpose(heads_out, (2, 0, 1, 3)).reshape(message_rows, local_heads * HD)
    product = jnp.dot(
        lax.all_gather(attention, "branch", axis=0, tiled=True),
        output_weight,
        preferred_element_type=jnp.float32,
    )
    partial_columns = product.astype(jnp.bfloat16).astype(jnp.float32)
    column_totals = lax.psum_scatter(
        partial_columns.astype(jnp.bfloat16), "tensor", scatter_dimension=1, tiled=True
    )
    result = lax.all_to_all(column_totals, "branch", split_axis=0, concat_axis=1, tiled=True)
    return result


def solution(mesh):
    return jax.shard_map(
        per_device,
        mesh=mesh,
        in_specs=(
            P(("group", "branch"), "tensor"),
            P(None, "group", "tensor"),
            P(None, ("group", "branch"), "tensor"),
            P(None, ("group", "branch"), "tensor"),
            P("group", None),
            P("group"),
            P("tensor", "branch"),
        ),
        out_specs=P(("group", "branch"), "tensor"),
        check_vma=False,
    )
```

profile of v0, /device:TPU:16, one launch (start us, length us, event | category | flops | bytes accessed | tf_op | source)
XLA Modules:
  0.0 345.3 jit_solution(16154351550768117709)
XLA Ops:
  10.8 18.8 %while.51 = (s32[]{:T(128)}, f32[1,8,256]{2,1,0:T(8,128)S(1)}, f32[1,8,256]{2,1,0:T(8,128)S(1)}, f32[1,8,256,128]{3,2,1,0:T(8,128)S(1)}, bf16[2,768,1,128]{3,1,2...) while((s32[]{:T(128)}, f32[1,8,256]{2,1,0:T(8,128)S(1)}, ...), condition=%wide.region_3.4_spmd.clone, body=%wide.region_0.3_spmd.clone.sunk | while | flops 818688000 | bytes 47186060 | solution.py:70
  10.8 3.6 %bitcast_reduce_fusion.5 = (f32[8,256]{1,0:T(8,128)S(1)}, f32[768,256,8]{1,0,2:T(8,128)}) fusion(bf16[256,1,8,128]{3,0,2,1:T(8,128)(2,1)S(1)} %get-tuple-element.758, bf16[2,768,1,128]{3,1,2,0:T(8,128)(2,1)S(1)} %get-tuple-element.757, s32[]{:T(128)} %get-tuple-element.744), kind=kOutput, calls=%fused_computation.88.clone.1 | convolution fusion | flops 405796864 | bytes 7020548 | tf_op jit(solution)/shard_map/while/body/eval_jaxpr/qhgd,khd->hgqk/dot_general | solution.py:24
  14.5 4.5 %fusion.130 = f32[1,8,256,128]{3,2,1,0:T(8,128)S(1)} fusion(f32[768,256,8]{1,0,2:T(8,128)} %get-tuple-element.733, f32[8,256]{1,0:T(8,128)S(1)} %bitcast.284, f32[1,8,256,128]{3,2,1,0:T(8,128)S(1)} %get-tuple-element.747, f32[8,256]{1,0:T(8,128)S(1)} %get-tuple-element.734, pred[]{:T(512)S(6)} %compare.35, ...), kind=kOutput, calls=%fused_computation.97.clone.1 | convolution fusion | flops 408158208 | bytes 8601605 | tf_op jit(solution)/shard_map/while/body/eval_jaxpr/hgqk,khd->hgqd/dot_general | solution.py:37
  20.1 3.6 %bitcast_reduce_fusion.5 = (f32[8,256]{1,0:T(8,128)S(1)}, f32[768,256,8]{1,0,2:T(8,128)}) fusion(bf16[256,1,8,128]{3,0,2,1:T(8,128)(2,1)S(1)} %get-tuple-element.758, bf16[2,768,1,128]{3,1,2,0:T(8,128)(2,1)S(1)} %get-tuple-element.757, s32[]{:T(128)} %get-tuple-element.744), kind=kOutput, calls=%fused_computation.88.clone.1 | convolution fusion | flops 405796864 | bytes 7020548 | tf_op jit(solution)/shard_map/while/body/eval_jaxpr/qhgd,khd->hgqk/dot_general | solution.py:24
  23.8 4.7 %fusion.130 = f32[1,8,256,128]{3,2,1,0:T(8,128)S(1)} fusion(f32[768,256,8]{1,0,2:T(8,128)} %get-tuple-element.733, f32[8,256]{1,0:T(8,128)S(1)} %bitcast.284, f32[1,8,256,128]{3,2,1,0:T(8,128)S(1)} %get-tuple-element.747, f32[8,256]{1,0:T(8,128)S(1)} %get-tuple-element.734, pred[]{:T(512)S(6)} %compare.35, ...), kind=kOutput, calls=%fused_computation.97.clone.1 | convolution fusion | flops 408158208 | bytes 8601605 | tf_op jit(solution)/shard_map/while/body/eval_jaxpr/hgqk,khd->hgqd/dot_general | solution.py:37
  30.9 33.1 %all-gather.4.cloned.1.call-done = bf16[2,4096,128]{2,1,0:T(8,128)(2,1)} async-done(((bf16[2,256,128]{2,1,0:T(8,128)(2,1)}), bf16[2,4096,128]{2,1,0:T(8,128)(2,1)}) %all-gather.4.cloned.1.call-update) | async-done | bytes 2097168 | tf_op jit(solution)/shard_map/all_gather | solution.py:133
  63.9 3.0 fusion.93
  67.0 42.6 %while.49 = (s32[]{:T(128)}, f32[1,8,256]{2,1,0:T(8,128)S(1)}, f32[1,8,256]{2,1,0:T(8,128)S(1)}, f32[1,8,256,128]{3,2,1,0:T(8,128)S(1)}, s32[4]{0:T(128)S(1)}, /...) while((s32[]{:T(128)}, f32[1,8,256]{2,1,0:T(8,128)S(1)}, ...), condition=%wide.region_8.9_spmd.clone, body=%wide.region_4.8_spmd.clone.sunk | while | flops 1101600768 | bytes 28465352 | solution.py:70
  70.8 4.2 %fusion.118 = f32[1,8,256,128]{3,2,1,0:T(8,128)S(1)} fusion(f32[1024,256,8]{1,0,2:T(8,128)S(1)} %get-tuple-element.705, f32[8,256]{1,0:T(8,128)S(1)} %bitcast.288, pred[1024]{0:T(1024)(128)(4,1)S(1)} %broadcast_compare_fusion.5, f32[1,8,256,128]{3,2,1,0:T(8,128)S(1)} %get-tuple-element.776, f32[8,256]{1,0:T(8,128)S(1)} %get-tuple-element.706, ...), kind=kOutput, calls=%fused_computation.15.clone.1 | convolution fusion | flops 547880960 | bytes 10766848 | tf_op jit(solution)/shard_map/while/body/eval_jaxpr/hgqk,khd->hgqd/dot_general | solution.py:37
  81.5 4.2 %fusion.118 = f32[1,8,256,128]{3,2,1,0:T(8,128)S(1)} fusion(f32[1024,256,8]{1,0,2:T(8,128)S(1)} %get-tuple-element.705, f32[8,256]{1,0:T(8,128)S(1)} %bitcast.288, pred[1024]{0:T(1024)(128)(4,1)S(1)} %broadcast_compare_fusion.5, f32[1,8,256,128]{3,2,1,0:T(8,128)S(1)} %get-tuple-element.776, f32[8,256]{1,0:T(8,128)S(1)} %get-tuple-element.706, ...), kind=kOutput, calls=%fused_computation.15.clone.1 | convolution fusion | flops 547880960 | bytes 10766848 | tf_op jit(solution)/shard_map/while/body/eval_jaxpr/hgqk,khd->hgqd/dot_general | solution.py:37
  85.6 2.6 fusion.117
  92.1 4.2 %fusion.118 = f32[1,8,256,128]{3,2,1,0:T(8,128)S(1)} fusion(f32[1024,256,8]{1,0,2:T(8,128)S(1)} %get-tuple-element.705, f32[8,256]{1,0:T(8,128)S(1)} %bitcast.288, pred[1024]{0:T(1024)(128)(4,1)S(1)} %broadcast_compare_fusion.5, f32[1,8,256,128]{3,2,1,0:T(8,128)S(1)} %get-tuple-element.776, f32[8,256]{1,0:T(8,128)S(1)} %get-tuple-element.706, ...), kind=kOutput, calls=%fused_computation.15.clone.1 | convolution fusion | flops 547880960 | bytes 10766848 | tf_op jit(solution)/shard_map/while/body/eval_jaxpr/hgqk,khd->hgqd/dot_general | solution.py:37
  102.8 4.2 %fusion.118 = f32[1,8,256,128]{3,2,1,0:T(8,128)S(1)} fusion(f32[1024,256,8]{1,0,2:T(8,128)S(1)} %get-tuple-element.705, f32[8,256]{1,0:T(8,128)S(1)} %bitcast.288, pred[1024]{0:T(1024)(128)(4,1)S(1)} %broadcast_compare_fusion.5, f32[1,8,256,128]{3,2,1,0:T(8,128)S(1)} %get-tuple-element.776, f32[8,256]{1,0:T(8,128)S(1)} %get-tuple-element.706, ...), kind=kOutput, calls=%fused_computation.15.clone.1 | convolution fusion | flops 547880960 | bytes 10766848 | tf_op jit(solution)/shard_map/while/body/eval_jaxpr/hgqk,khd->hgqd/dot_general | solution.py:37
  109.6 9.5 %all-gather.6.cloned.1.call-done = bf16[2,4096,128]{2,1,0:T(8,128)(2,1)} async-done(((bf16[2,256,128]{2,1,0:T(8,128)(2,1)}), bf16[2,4096,128]{2,1,0:T(8,128)(2,1)}) %all-gather.6.cloned.1.call-update) | async-done | bytes 2097168 | tf_op jit(solution)/shard_map/all_gather | solution.py:134
  119.1 3.0 fusion.92
  122.2 44.2 %while.50 = (s32[]{:T(128)}, f32[1,8,256]{2,1,0:T(8,128)S(1)}, f32[1,8,256]{2,1,0:T(8,128)S(1)}, f32[1,8,256,128]{3,2,1,0:T(8,128)S(1)}, s32[4]{0:T(128)S(1)}, /...) while((s32[]{:T(128)}, f32[1,8,256]{2,1,0:T(8,128)S(1)}, ...), condition=%wide.region_13.14_spmd.clone, body=%wide.region_9.13_spmd.clone.sunk | while | flops 1102416896 | bytes 29521128 | solution.py:70
  127.4 3.7 %fusion.125 = f32[1,8,256,128]{3,2,1,0:T(8,128)S(1)} fusion(f32[1024,256,8]{1,0,2:T(8,128)S(1)} %get-tuple-element.722, f32[8,256]{1,0:T(8,128)S(1)} %bitcast.290, pred[256,1024]{0,1:T(8,128)(4,1)S(1)} %fusion.121, f32[1,8,256,128]{3,2,1,0:T(8,128)S(1)} %get-tuple-element.811, f32[8,256]{1,0:T(8,128)S(1)} %get-tuple-element.723, ...), kind=kOutput, calls=%fused_computation.52.clone.1 | convolution fusion | flops 547880960 | bytes 11026944 | tf_op jit(solution)/shard_map/while/body/eval_jaxpr/hgqk,khd->hgqd/dot_general | solution.py:37
  138.5 3.7 %fusion.125 = f32[1,8,256,128]{3,2,1,0:T(8,128)S(1)} fusion(f32[1024,256,8]{1,0,2:T(8,128)S(1)} %get-tuple-element.722, f32[8,256]{1,0:T(8,128)S(1)} %bitcast.290, pred[256,1024]{0,1:T(8,128)(4,1)S(1)} %fusion.121, f32[1,8,256,128]{3,2,1,0:T(8,128)S(1)} %get-tuple-element.811, f32[8,256]{1,0:T(8,128)S(1)} %get-tuple-element.723, ...), kind=kOutput, calls=%fused_computation.52.clone.1 | convolution fusion | flops 547880960 | bytes 11026944 | tf_op jit(solution)/shard_map/while/body/eval_jaxpr/hgqk,khd->hgqd/dot_general | solution.py:37
  149.6 3.7 %fusion.125 = f32[1,8,256,128]{3,2,1,0:T(8,128)S(1)} fusion(f32[1024,256,8]{1,0,2:T(8,128)S(1)} %get-tuple-element.722, f32[8,256]{1,0:T(8,128)S(1)} %bitcast.290, pred[256,1024]{0,1:T(8,128)(4,1)S(1)} %fusion.121, f32[1,8,256,128]{3,2,1,0:T(8,128)S(1)} %get-tuple-element.811, f32[8,256]{1,0:T(8,128)S(1)} %get-tuple-element.723, ...), kind=kOutput, calls=%fused_computation.52.clone.1 | convolution fusion | flops 547880960 | bytes 11026944 | tf_op jit(solution)/shard_map/while/body/eval_jaxpr/hgqk,khd->hgqd/dot_general | solution.py:37
  160.6 3.7 %fusion.125 = f32[1,8,256,128]{3,2,1,0:T(8,128)S(1)} fusion(f32[1024,256,8]{1,0,2:T(8,128)S(1)} %get-tuple-element.722, f32[8,256]{1,0:T(8,128)S(1)} %bitcast.290, pred[256,1024]{0,1:T(8,128)(4,1)S(1)} %fusion.121, f32[1,8,256,128]{3,2,1,0:T(8,128)S(1)} %get-tuple-element.811, f32[8,256]{1,0:T(8,128)S(1)} %get-tuple-element.723, ...), kind=kOutput, calls=%fused_computation.52.clone.1 | convolution fusion | flops 547880960 | bytes 11026944 | tf_op jit(solution)/shard_map/while/body/eval_jaxpr/hgqk,khd->hgqd/dot_general | solution.py:37
  169.9 84.2 %all-gather.8.cloned.1.call-done = bf16[4096,1024]{0,1:T(8,128)(2,1)} async-done(((bf16[256,1024]{0,1:T(8,128)(2,1)}), bf16[4096,1024]{0,1:T(8,128)(2,1)}) %all-gather.8.cloned.1.call-update) | async-done | bytes 8388624 | tf_op jit(solution)/shard_map/all_gather | solution.py:141
  254.1 9.5 %convolution_convert_fusion = bf16[4096,512]{0,1:T(8,128)(2,1)} fusion(bf16[4096,1024]{0,1:T(8,128)(2,1)} %all-gather.8.cloned.1.call-done, bf16[1024,512]{1,0:T(8,128)(2,1)S(1)} %copy-done), kind=kOutput, calls=%fused_computation.113 | convolution fusion | flops 4297064448 | bytes 13631488 | tf_op jit(solution)/shard_map/dot_general | solution.py:140
  263.7 56.5 %reduce-scatter.2.cloned.1.call-done = bf16[4096,64]{0,1:T(8,128)(2,1)} async-done(((bf16[4096,512]{0,1:T(8,128)(2,1)}), bf16[4096,64]{0,1:T(8,128)(2,1)}) %reduce-scatter.2.cloned.1.call-update) | async-done | bytes 524304 | tf_op jit(solution)/shard_map/reduce_scatter | solution.py:146
  321.2 16.5 %all_to_all.19 = bf16[16,256,64]{1,2,0:T(8,128)(2,1)S(1)} all-to-all(bf16[16,256,64]{1,2,0:T(8,128)(2,1)S(1)} %bitcast.294), channel_id=1, replica_groups=mesh['group'=2,'branch'=16,'tensor'=8] {'branch'}, dimensions={0} | all-to-all | bytes 1048576 | tf_op jit(solution)/shard_map/all_to_all | solution.py:149
  (117 shorter events, 60.6 us)
Async XLA Ops:
  6.5 247.6 %copy-start = (bf16[1024,512]{1,0:T(8,128)(2,1)S(1)}, bf16[1024,512]{1,0:T(8,128)(2,1)}, u32[]{:S(2)}) copy-start(bf16[1024,512]{1,0:T(8,128)(2,1)} %param.19) | copy-start | bytes 3145732
  6.5 57.4 %all-gather.4.cloned.1.call-start = ((), (), s32[]{:S(2)}) async-start(), calls=%async_computation.2 | async-start | bytes 2228224 | tf_op jit(solution)/shard_map/all_gather | solution.py:133
  7.3 111.9 %all-gather.6.cloned.1.call-start = ((), (), s32[]{:S(2)}) async-start(), calls=%async_computation.3 | async-start | bytes 2228224 | tf_op jit(solution)/shard_map/all_gather | solution.py:134
  8.0 246.1 %all-gather.8.cloned.1.call-start = ((), (), s32[]{:S(2)}) async-start(), calls=%async_computation.4 | async-start | bytes 8912896 | tf_op jit(solution)/shard_map/all_gather | solution.py:141
  10.8 19.5 %copy-start.2 = (s32[16]{0:T(128)S(1)}, s32[16]{0:T(128)}, u32[]{:S(2)}) copy-start(s32[16]{0:T(128)} %param.18) | copy-start | bytes 196
  14.4 4.6 %copy-start.1 = (f32[768,256,8]{1,0,2:T(8,128)S(1)}, f32[768,256,8]{1,0,2:T(8,128)}, u32[]{:S(2)}) copy-start(f32[768,256,8]{1,0,2:T(8,128)} %get-tuple-element.733) | copy-start | bytes 18874372 | tf_op jit(solution)/shard_map/while
  23.8 4.8 %copy-start.1 = (f32[768,256,8]{1,0,2:T(8,128)S(1)}, f32[768,256,8]{1,0,2:T(8,128)}, u32[]{:S(2)}) copy-start(f32[768,256,8]{1,0,2:T(8,128)} %get-tuple-element.733) | copy-start | bytes 18874372 | tf_op jit(solution)/shard_map/while
  169.8 150.3 %reduce-scatter.2.cloned.1.call-start = ((), (), s32[]{:S(2)}) async-start(), calls=%async_computation.5 | async-start | bytes 4718592 | tf_op jit(solution)/shard_map/reduce_scatter | solution.py:146
Sparse Core Ops, SparseCore 0:
  10.1 53.7 all-gather.3
  66.7 52.3 all-gather.5
  169.9 84.0 all-gather.7
  263.8 56.2 reduce-scatter.1
where the time goes:
time: 349 us; the launch traced here: 345 us
  waiting for transfers between devices  185 us (53%)
  matrix products  77.1 us (22%)
  other arithmetic  29.6 us (8%)
  local copies, waits for them, and re-layouts  18.5 us (5%)
  blocking collectives  16.5 us (5%)
  between operations  13.2 us (4%)
  loops' own time  5.53 us (2%)
    all_gather x1, waiting for transfers between devices, per_device(): lax.all_gather(attention, 'branch', axis=0, tiled=True)  84.2 us
    reduce_scatter x1, waiting for transfers between devices, per_device(): lax.psum_scatter(partial_columns.astype(jnp.bfloat16), 'tensor', scatter_...  56.5 us
    dot_general x10, matrix products, update_state(): jnp.einsum('hgqk,khd->hgqd', weights.astype(jnp.bfloat16), value_rows, pr...  40.7 us
    all_gather x1, waiting for transfers between devices, per_device(): lax.all_gather(prior_cache, 'branch', axis=1, tiled=True)  33.1 us
    dot_general x10, matrix products, update_state(): jnp.einsum('qhgd,khd->hgqk', query_heads, key_rows, preferred_element_typ...  26.8 us
    reduce_sum x10, other arithmetic, update_state(): total_new = total_old * factor + jnp.sum(weights, axis=-1)  20.4 us
    all_to_all x1, blocking collectives, per_device(): lax.all_to_all(column_totals, 'branch', split_axis=0, concat_axis=1, tile...  16.5 us
    dot_general x1, matrix products, per_device(): jnp.dot(lax.all_gather(attention, 'branch', axis=0, tiled=True), output_w...  9.54 us
  transfers between devices with their start and end apart: 4, of which 4 were waited for; matrix products, arithmetic and copies ran while one was open for 19% of the time, Pallas kernels for 0%

commit v1 on v0

v1 whole, which is shorter than its diff:
```python
import math

import jax
import jax.numpy as jnp
from jax import lax
from jax.experimental import pallas as pl
from jax.experimental.pallas import tpu as pltpu
from jax.sharding import PartitionSpec as P

MESH = pl.DeviceIdType.MESH
HD = 128
HEADS = 8
MSG = 256
PREFIX = 1536
CH = 4
ROWS = MSG // CH
QT = ROWS * HEADS
TR = 8
ST = 2 * CH
LAST = 3
SCALE = math.log2(math.e) / math.sqrt(HD)
BIG = 1e30
BF = jnp.bfloat16
F32 = jnp.float32


def dg(a, b, ca, cb):
    return lax.dot_general(a, b, (((ca,), (cb,)), ((), ())), preferred_element_type=F32)


def pick(index, values):
    result = jnp.int32(values[0])
    for i in range(1, len(values)):
        result = jnp.where(index == i, jnp.int32(values[i]), result)
    return result


def kernel(q_ref, pre_ref, pri_ref, fre_ref, vis_ref, turn_ref, w_ref, o_ref,
           qs, pvt, kv, m, acc, ag, wraw, w4, part, rbuf, sbuf, stage,
           kv_s, kv_r, kf_s, kc_s, kc_r, w_s, w_r, wl_s, a_s, a_r, rs_s, rs_r, f_s, f_r):
    b = lax.axis_index("branch")
    z = lax.axis_index("tensor")
    c = lax.rem(b, 2)
    x = lax.rem(b // 2, 4)
    yh = b // 8
    chip = b // 2

    def dev(dy, dx, dc, dz=0):
        ny, nx, nc = lax.rem(yh + dy, 2), lax.rem(x + dx, 4), lax.rem(c + dc, 2)
        return {"branch": (ny * 4 + nx) * 2 + nc, "tensor": lax.rem(z + dz, TR)}

    def chip_at(dy, dx):
        return lax.rem(yh + dy, 2) * 4 + lax.rem(x + dx, 4)

    def remote(src, dst, ss, rs, to):
        return pltpu.make_async_remote_copy(src_ref=src, dst_ref=dst, send_sem=ss, recv_sem=rs,
                                            device_id=to, device_id_type=MESH)

    def put_tile(dst_rows, src):
        kv[chip, c, pl.ds(dst_rows, 128), :] = src

    kv[chip, c, 0:256, :] = pri_ref[0]
    kv[chip, c, 256:512, :] = fre_ref[0]
    for i in range(2):
        kv[chip, c, 512 + i * 128:640 + i * 128, :] = pri_ref[1, i * 128:(i + 1) * 128, :].astype(F32).T.astype(BF)
        kv[chip, c, 768 + i * 128:896 + i * 128, :] = fre_ref[1, i * 128:(i + 1) * 128, :].astype(F32).T.astype(BF)

    barrier = pltpu.get_barrier_semaphore()
    peers = [dev(0, 0, 1), dev(0, 1, 0), dev(0, 3, 0), dev(0, 2, 0), dev(1, 0, 0), dev(0, 0, 0, 1), dev(0, 0, 0, TR - 1)]
    for peer in peers:
        pl.semaphore_signal(barrier, inc=1, device_id=peer, device_id_type=MESH)
    pl.semaphore_wait(barrier, len(peers))

    def kv_send(i):
        to = [dev(0, 1, 0), dev(0, 3, 0), dev(1, 0, 0), dev(0, 2, 0)][i]
        return remote(kv.at[chip, c], kv.at[chip, c], kv_s.at[i], kv_r.at[chip], to)

    across = chip_at(1, 0)

    def kv_forward(i):
        to = [dev(0, 1, 0), dev(0, 3, 0), dev(0, 2, 0)][i]
        return remote(kv.at[across, c], kv.at[across, c], kf_s.at[i], kv_r.at[across], to)

    def kv_arrival(slot):
        return remote(kv.at[slot, c], kv.at[slot, c], kv_s.at[0], kv_r.at[slot], dev(0, 1, 0))

    def core_send(slot):
        return remote(kv.at[slot, c], kv.at[slot, c], kc_s.at[slot], kc_r.at[slot], dev(0, 0, 1))

    def core_arrival(slot):
        return remote(kv.at[slot, 1 - c], kv.at[slot, 1 - c], kc_s.at[slot], kc_r.at[slot], dev(0, 0, 1))

    core_send(chip).start()
    kv_send(0).start()
    kv_send(1).start()
    kv_send(2).start()

    own_w = yh * 2 + c
    far_w = (1 - yh) * 2 + c
    w_local = pltpu.make_async_copy(w_ref, wraw.at[own_w], wl_s.at[0])
    w_across = remote(w_ref, wraw.at[own_w], w_s.at[0], w_r.at[0], dev(1, 0, 0))
    w_core = remote(w_ref, wraw.at[own_w], w_s.at[1], w_r.at[1], dev(0, 0, 1))
    w_pass = remote(wraw.at[far_w], wraw.at[far_w], w_s.at[2], w_r.at[2], dev(0, 0, 1))
    w_local.start()

    for j in range(CH):
        for h in range(HEADS):
            qs[j, h * ROWS:(h + 1) * ROWS, :] = q_ref[j * ROWS:(j + 1) * ROWS, h * HD:(h + 1) * HD]
    for i in range(PREFIX // 128):
        pvt[i] = pre_ref[1, i * 128:(i + 1) * 128, :].astype(F32).T.astype(BF)
    m[...] = jnp.full(m.shape, -BIG, F32)
    acc[...] = jnp.zeros(acc.shape, F32)

    def scores(keys, j):
        return dg(keys, qs[j], 1, 1)

    def with_ones(tiles):
        values = jnp.concatenate(tiles, axis=1)
        return jnp.concatenate([values, jnp.ones((16, values.shape[1]), BF)], axis=0)

    def soften(j, s, values, sections):
        old = m[j]
        new = old
        parts = []
        for start, size, penalty, limit in sections:
            sec = s[start:start + size]
            if limit is not None:
                row = lax.broadcasted_iota(jnp.int32, sec.shape, 0)
                sec = jnp.where(row <= limit, sec, -BIG)
            top = jnp.max(sec, axis=0, keepdims=True) * SCALE
            if penalty is not None:
                top = top - penalty
            new = jnp.maximum(new, top)
            parts.append((sec, penalty))
        weights = []
        for sec, penalty in parts:
            shift = new if penalty is None else new + penalty
            weights.append(jnp.exp2(sec * SCALE - shift).astype(BF))
        p = weights[0] if len(weights) == 1 else jnp.concatenate(weights, axis=0)
        m[j] = new
        acc[j] = acc[j] * jnp.exp2(old - new) + dg(values, p, 1, 0)

    def sweep(keys, values, sections_of):
        ahead = scores(keys, 0)
        for j in range(CH):
            s = ahead
            if j + 1 < CH:
                ahead = scores(keys, j + 1)
            soften(j, s, values, sections_of(j))

    my_turn = turn_ref[b]

    def chip_keys(slot):
        return jnp.concatenate([kv[slot, 0, 0:512, :], kv[slot, 1, 0:512, :]], axis=0)

    def chip_values(slot):
        return with_ones([kv[slot, cc, 512 + 128 * i:640 + 128 * i, :] for cc in range(2) for i in range(4)])

    def chip_sections(slot, limits=None):
        out = []
        for cc in range(2):
            owner = slot * 2 + cc
            unseen = jnp.where(vis_ref[b, owner] == 1, 0.0, BIG)
            early = turn_ref[owner] < my_turn
            if limits is not None:
                early = early | (owner == b)
            later = jnp.where(early, 0.0, BIG)
            out.append((cc * 512, 256, unseen, None))
            out.append((cc * 512 + 256, 256, later, None if limits is None else limits[cc]))
        return out

    sweep(pre_ref[0], with_ones([pvt[i] for i in range(PREFIX // 128)]), lambda j: [(0, PREFIX, None, None)])

    kv_send(3).start()
    kv_arrival(across).wait_recv()
    kv_forward(0).start()
    kv_forward(1).start()
    core_send(across).start()
    w_core.start()
    w_across.start()
    core_arrival(chip).wait_recv()

    def own_sections(j):
        position = lax.rem(lax.broadcasted_iota(jnp.int32, (1, QT), 1), ROWS) + j * ROWS
        limits = [position + jnp.where(chip * 2 + cc == b, 0, MSG) for cc in range(2)]
        return chip_sections(chip, limits)

    sweep(chip_keys(chip), chip_values(chip), own_sections)
    kv_forward(2).start()

    order = [(0, 1), (0, 3), (1, 0), (0, 2), (1, 1), (1, 3), (1, 2)]
    FIRST = len(order) - LAST

    def slot_of(s):
        return chip_at(pick(s, [p[0] for p in order]), pick(s, [p[1] for p in order]))

    def fetch(s):
        @pl.when(s != 2)
        def _():
            slot = slot_of(s)
            kv_arrival(slot).wait_recv()
            core_send(slot).start()

    fetch(jnp.int32(0))

    def first_part(s, carry):
        slot = slot_of(s)
        fetch(s + 1)
        core_arrival(slot).wait_recv()
        sweep(chip_keys(slot), chip_values(slot), lambda j: chip_sections(slot))
        return carry

    lax.fori_loop(0, FIRST, first_part, 0)

    for s in range(FIRST + 1, len(order)):
        fetch(jnp.int32(s))
    for s in range(FIRST, len(order)):
        core_arrival(slot_of(jnp.int32(s))).wait_recv()

    def arrange(y):
        def some_rows(i, carry):
            rows = pl.ds(pl.multiple_of(i * 128, 128), 128)
            for u in range(4):
                low = wraw[y * 2, rows, u * 128:(u + 1) * 128]
                high = wraw[y * 2 + 1, rows, u * 128:(u + 1) * 128]
                w4[y, rows, u * 256:u * 256 + 128] = jnp.concatenate([low[:, :64], high[:, :64]], axis=1)
                w4[y, rows, u * 256 + 128:u * 256 + 256] = jnp.concatenate([low[:, 64:], high[:, 64:]], axis=1)
            return carry
        lax.fori_loop(0, 8, some_rows, 0)

    w_local.wait()
    w_core.wait_recv()
    arrange(yh)

    def a_send(j, r):
        return remote(ag.at[j, x], ag.at[j, x], a_s.at[j, r - 1], a_r.at[j, r - 1], dev(0, r, 0))

    last_slots = [slot_of(jnp.int32(s)) for s in range(FIRST, len(order))]

    def second_part(j, carry):
        ahead = scores(chip_keys(last_slots[0]), j)
        for n in range(LAST):
            s = ahead
            if n + 1 < LAST:
                ahead = scores(chip_keys(last_slots[n + 1]), j)
            soften(j, s, chip_values(last_slots[n]), chip_sections(last_slots[n]))
        done = acc[j]
        heads = (done[:HD] / done[HD:HD + 1]).T.astype(BF)
        for h in range(HEADS):
            ag[j, x, :, h * HD:(h + 1) * HD] = heads[h * ROWS:(h + 1) * ROWS, :]
        for r in (1, 3, 2):
            a_send(j, r).start()

        @pl.when(j == CH - 2)
        def _():
            w_across.wait_recv()
            w_pass.start()

        return carry

    lax.fori_loop(0, CH, second_part, 0)

    def ring_copy(st, s, d):
        to = dev(0, 0, 0, 1 if d == 0 else TR - 1)
        return remote(sbuf.at[st, s, d], rbuf.at[st, s, d], rs_s.at[st, s, d], rs_r.at[st, s, d], to)

    def target(s, d):
        return lax.rem(z + 2 * TR - 1 - s, TR) if d == 0 else lax.rem(z + 1 + s, TR)

    def final_send(st, r):
        j, y = st // 2, lax.rem(yh + st, 2)
        spot = o_ref.at[pl.ds(pl.multiple_of(j * ROWS, ROWS), ROWS), pl.ds(pl.multiple_of((y * 4 + x) * 128, 128), 128)]
        return remote(stage.at[st, lax.rem(x + r, 4)], spot, f_s.at[st, r - 1], f_r.at[st, r - 1], dev(0, r, 0))

    def final_arrival(st, r):
        j, y = st // 2, lax.rem(yh + st, 2)
        source = lax.rem(x + 4 - r, 4)
        spot = o_ref.at[pl.ds(pl.multiple_of(j * ROWS, ROWS), ROWS), pl.ds(pl.multiple_of((y * 4 + source) * 128, 128), 128)]
        return remote(stage.at[st, 0], spot, f_s.at[st, r - 1], f_r.at[st, r - 1], dev(0, r, 0))

    def begin(st):
        j, y = st // 2, lax.rem(yh + st, 2)

        @pl.when(lax.rem(st, 2) == 0)
        def _():
            for r in (1, 3, 2):
                source = lax.rem(x + 4 - r, 4)
                remote(ag.at[j, source], ag.at[j, source], a_s.at[j, r - 1], a_r.at[j, r - 1], dev(0, r, 0)).wait_recv()

        @pl.when(st == 1)
        def _():
            w_pass.wait_recv()
            arrange(1 - yh)

        left = ag[j].reshape(4 * ROWS, HEADS * HD)
        for u in range(4):
            product = dg(left, w4[y, :, u * 256:(u + 1) * 256], 1, 0).astype(BF)
            part[st, 2 * u] = product[:, :128]
            part[st, 2 * u + 1] = product[:, 128:]
        for d in range(2):
            sbuf[st, 0, d] = part[st, target(0, d), d * 128:(d + 1) * 128, :]
            ring_copy(st, 0, d).start()

    def middle(st, s):
        for d in range(2):
            ring_copy(st, s - 1, d).wait_recv()
            total = rbuf[st, s - 1, d].astype(F32) + part[st, target(s, d), d * 128:(d + 1) * 128, :].astype(F32)
            sbuf[st, s, d] = total.astype(BF)
            ring_copy(st, s, d).start()

    def finish(st):
        j, y = st // 2, lax.rem(yh + st, 2)
        for d in range(2):
            ring_copy(st, TR - 2, d).wait_recv()
            total = rbuf[st, TR - 2, d].astype(F32) + part[st, z, d * 128:(d + 1) * 128, :].astype(F32)
            stage[st, 2 * d:2 * d + 2] = total.astype(BF).reshape(2, ROWS, 128)
        for r in (1, 3, 2):
            final_send(st, r).start()
        o_ref[pl.ds(pl.multiple_of(j * ROWS, ROWS), ROWS), pl.ds(pl.multiple_of((y * 4 + x) * 128, 128), 128)] = stage[st, x]

    def tick(T, carry):
        def one(st, inner):
            s = T - st

            @pl.when(s == 0)
            def _():
                begin(st)

            @pl.when((s >= 1) & (s < TR - 1))
            def _():
                middle(st, s)

            @pl.when(s == TR - 1)
            def _():
                finish(st)

            return inner

        return lax.fori_loop(0, ST, one, carry)

    lax.fori_loop(0, ST + TR - 1, tick, 0)

    def drain(st, carry):
        for r in (1, 2, 3):
            final_arrival(st, r).wait_recv()
            final_send(st, r).wait_send()
        return carry

    lax.fori_loop(0, ST, drain, 0)

    def drain_ring(n, carry):
        for d in range(2):
            ring_copy(n // (TR - 1), lax.rem(n, TR - 1), d).wait_send()
        return carry

    lax.fori_loop(0, ST * (TR - 1), drain_ring, 0)

    def drain_heads(j, carry):
        for r in (1, 2, 3):
            a_send(j, r).wait_send()
        return carry

    lax.fori_loop(0, CH, drain_heads, 0)
    for i in range(4):
        kv_send(i).wait_send()
    for i in range(3):
        kv_forward(i).wait_send()

    def drain_core(slot, carry):
        core_send(slot).wait_send()
        return carry

    lax.fori_loop(0, 8, drain_core, 0)
    w_across.wait_send()
    w_core.wait_send()
    w_pass.wait_send()


def per_device(queries, prefix_cache, prior_cache, fresh_cache, visible, turn_order, output_weight):
    vm = pl.BlockSpec(memory_space=pltpu.VMEM)
    sm = pl.BlockSpec(memory_space=pltpu.SMEM)
    dma = pltpu.SemaphoreType.DMA
    return pl.pallas_call(
        kernel,
        name="debate",
        out_shape=jax.ShapeDtypeStruct(queries.shape, BF),
        in_specs=[vm, vm, vm, vm, sm, sm, vm],
        out_specs=vm,
        scratch_shapes=[
            pltpu.VMEM((CH, QT, HD), BF),
            pltpu.VMEM((PREFIX // 128, 128, 128), BF),
            pltpu.VMEM((8, 2, 1024, HD), BF),
            pltpu.VMEM((CH, 1, QT), F32),
            pltpu.VMEM((CH, HD + 16, QT), F32),
            pltpu.VMEM((CH, 4, ROWS, HEADS * HD), BF),
            pltpu.VMEM((4, 1024, 512), BF),
            pltpu.VMEM((2, 1024, 1024), BF),
            pltpu.VMEM((ST, TR, 4 * ROWS, 128), BF),
            pltpu.VMEM((ST, TR - 1, 2, 2 * ROWS, 128), BF),
            pltpu.VMEM((ST, TR - 1, 2, 2 * ROWS, 128), BF),
            pltpu.VMEM((ST, 4, ROWS, 128), BF),
            dma((4,)), dma((8,)), dma((3,)), dma((8,)), dma((8,)),
            dma((3,)), dma((3,)), dma((1,)),
            dma((CH, 3)), dma((CH, 3)),
            dma((ST, TR - 1, 2)), dma((ST, TR - 1, 2)),
            dma((ST, 3)), dma((ST, 3)),
        ],
        compiler_params=pltpu.CompilerParams(collective_id=0, has_side_effects=True, vmem_limit_bytes=60 << 20),
        cost_estimate=pl.CostEstimate(flops=15_000_000_000, bytes_accessed=6_000_000, transcendentals=20_000_000),
    )(queries, prefix_cache, prior_cache, fresh_cache, visible, turn_order, output_weight)


def solution(mesh):
    return jax.shard_map(
        per_device,
        mesh=mesh,
        in_specs=(
            P(("group", "branch"), "tensor"),
            P(None, "group", "tensor"),
            P(None, ("group", "branch"), "tensor"),
            P(None, ("group", "branch"), "tensor"),
            P("group", None),
            P("group"),
            P("tensor", "branch"),
        ),
        out_specs=P(("group", "branch"), "tensor"),
        check_vma=False,
    )
```

time: 349 us -> 121 us (0.35); the launches traced: 345 us -> 121 us
  waiting for transfers between devices: 185 us -> 0 us
  Pallas kernels: 0 us -> 119 us
  matrix products: 77.1 us -> 0 us
  other arithmetic: 29.6 us -> 0 us
  local copies, waits for them, and re-layouts: 18.5 us -> 1.87 us
  blocking collectives: 16.5 us -> 0 us
  between operations: 13.2 us -> 0.01 us
  loops' own time: 5.53 us -> 0 us
    all_gather x3 -> x0, waiting for transfers between devices: 127 us -> none  [the longest x1 84.2 us: per_device(): lax.all_gather(attention, 'branch', axis=0, tiled=True)]
    pallas_call x0 -> x1, Pallas kernels: none -> 119 us  [per_device(): pl.pallas_call(kernel, name='debate', out_shape=jax.ShapeDtypeStruct(quer...]
    dot_general x21 -> x0, matrix products: 77.1 us -> none  [the longest x10 40.7 us: update_state(): jnp.einsum('hgqk,khd->hgqd', weights.astype(jnp.bfloat16), value_rows, pr...]
    reduce_scatter x1 -> x0, waiting for transfers between devices: 56.5 us -> none  [per_device(): lax.psum_scatter(partial_columns.astype(jnp.bfloat16), 'tensor', scatter_...]
    reduce_sum x18 -> x0, other arithmetic: 21.1 us -> none  [the longest x10 20.4 us: update_state(): total_new = total_old * factor + jnp.sum(weights, axis=-1)]
    all_to_all x1 -> x0, blocking collectives: 16.5 us -> none  [per_device(): lax.all_to_all(column_totals, 'branch', split_axis=0, concat_axis=1, tile...]
    slice x3 -> x0, local copies, waits for them, and re-layouts: 7.21 us -> none  [split_cache(): cache[1].reshape(-1, local_groups, HD)]
    dynamic_slice x10 -> x0, local copies, waits for them, and re-layouts: 6.17 us -> none  [the longest x8 4.92 us: sweep(): lax.scan(advance, running, (key_blocks, value_blocks, jnp.arange(block_co...]
  transfers between devices with their start and end apart: 4 -> 0, of which waited for: 4 -> 0; matrix products, arithmetic and copies ran while one was open for 19% -> 0% of each run, Pallas kernels for 0% -> 0%
where the time goes in v1:
time: 121 us
  Pallas kernels  119 us (98%)
  local copies, waits for them, and re-layouts  1.87 us (2%)
    pallas_call x1, Pallas kernels, per_device(): pl.pallas_call(kernel, name='debate', out_shape=jax.ShapeDtypeStruct(quer...  119 us

profile of v1, /device:TPU:16, one launch (start us, length us, event | category | flops | bytes accessed | tf_op | source)
XLA Modules:
  0.0 120.8 jit_solution(13115928839850485971)
XLA Ops:
  0.0 119.0 %debate.1 = bf16[256,1024]{1,0:T(8,128)(2,1)} custom-call(bf16[256,1024]{1,0:T(8,128)(2,1)} %q_ref.1, bf16[2,1536,128]{2,1,0:T(8,128)(2,1)} %pre_ref.1, bf16[2,256,128]{2,1,0:T(8,128)(2,1)} %pri_ref.1, bf16[2,256,128]{2,1,0:T(8,128)(2,1)} %fre_ref.1, s32[16,16]{1,0:T(8,128)} %vis_ref.1, s32[16]{0:T(128)} %turn_ref.1, bf16[1024,512]{1,0:T(8,128)(2,1)} %w_ref.1), custom_call_target="tpu_custom_call" | custom-call | flops 15000000512 | bytes 6000000 | tf_op jit(solution)/shard_map/debate/pallas_call | solution.py:383
  119.0 1.9 %copy.9 = bf16[256,1024]{1,0:T(8,128)(2,1)} copy(bf16[256,1024]{1,0:T(8,128)(2,1)} %debate.1) | data formatting | bytes 1048576

commit v2 on v1

--- a/solution.py
+++ b/solution.py
@@ -17,7 +17,7 @@
 QT = ROWS * HEADS
 TR = 8
 ST = 2 * CH
-LAST = 3
+START = (0, 1, 2, 2, 2, 3, 3, 3)
 SCALE = math.log2(math.e) / math.sqrt(HD)
 BIG = 1e30
 BF = jnp.bfloat16
@@ -37,7 +37,7 @@
 
 def kernel(q_ref, pre_ref, pri_ref, fre_ref, vis_ref, turn_ref, w_ref, o_ref,
            qs, pvt, kv, m, acc, ag, wraw, w4, part, rbuf, sbuf, stage,
-           kv_s, kv_r, kf_s, kc_s, kc_r, w_s, w_r, wl_s, a_s, a_r, rs_s, rs_r, f_s, f_r):
+           kv_s, kv_r, kf_s, kh_s, kh_r, kc_s, kc_r, w_s, w_r, wl_s, a_s, a_r, rs_s, rs_r, f_s, f_r):
     b = lax.axis_index("branch")
     z = lax.axis_index("tensor")
     c = lax.rem(b, 2)
@@ -56,8 +56,10 @@
         return pltpu.make_async_remote_copy(src_ref=src, dst_ref=dst, send_sem=ss, recv_sem=rs,
                                             device_id=to, device_id_type=MESH)
 
-    def put_tile(dst_rows, src):
-        kv[chip, c, pl.ds(dst_rows, 128), :] = src
+    barrier = pltpu.get_barrier_semaphore()
+    peers = [dev(0, 0, 1), dev(0, 1, 0), dev(0, 3, 0), dev(0, 2, 0), dev(1, 0, 0), dev(0, 0, 0, 1), dev(0, 0, 0, TR - 1)]
+    for peer in peers:
+        pl.semaphore_signal(barrier, inc=1, device_id=peer, device_id_type=MESH)
 
     kv[chip, c, 0:256, :] = pri_ref[0]
     kv[chip, c, 256:512, :] = fre_ref[0]
@@ -65,42 +67,49 @@
         kv[chip, c, 512 + i * 128:640 + i * 128, :] = pri_ref[1, i * 128:(i + 1) * 128, :].astype(F32).T.astype(BF)
         kv[chip, c, 768 + i * 128:896 + i * 128, :] = fre_ref[1, i * 128:(i + 1) * 128, :].astype(F32).T.astype(BF)
 
-    barrier = pltpu.get_barrier_semaphore()
-    peers = [dev(0, 0, 1), dev(0, 1, 0), dev(0, 3, 0), dev(0, 2, 0), dev(1, 0, 0), dev(0, 0, 0, 1), dev(0, 0, 0, TR - 1)]
-    for peer in peers:
-        pl.semaphore_signal(barrier, inc=1, device_id=peer, device_id_type=MESH)
-    pl.semaphore_wait(barrier, len(peers))
+    across = chip_at(1, 0)
+    right, left = dev(0, 1, 0), dev(0, 3, 0)
+    right_chip, left_chip, far_chip = chip_at(0, 1), chip_at(0, 3), chip_at(0, 2)
+    right_across, left_across, far_across = chip_at(1, 1), chip_at(1, 3), chip_at(1, 2)
+    halves = (pl.ds(0, 512), pl.ds(512, 512))
 
     def kv_send(i):
-        to = [dev(0, 1, 0), dev(0, 3, 0), dev(1, 0, 0), dev(0, 2, 0)][i]
+        to = [right, left, dev(1, 0, 0)][i]
         return remote(kv.at[chip, c], kv.at[chip, c], kv_s.at[i], kv_r.at[chip], to)
 
-    across = chip_at(1, 0)
-
     def kv_forward(i):
-        to = [dev(0, 1, 0), dev(0, 3, 0), dev(0, 2, 0)][i]
-        return remote(kv.at[across, c], kv.at[across, c], kf_s.at[i], kv_r.at[across], to)
+        return remote(kv.at[across, c], kv.at[across, c], kf_s.at[i], kv_r.at[across], [right, left][i])
 
     def kv_arrival(slot):
-        return remote(kv.at[slot, c], kv.at[slot, c], kv_s.at[0], kv_r.at[slot], dev(0, 1, 0))
+        return remote(kv.at[slot, c], kv.at[slot, c], kv_s.at[0], kv_r.at[slot], right)
+
+    def kv_relay(row, half):
+        slot = [[left_chip, right_chip], [left_across, right_across]][row][half]
+        spot = kv.at[slot, c, halves[half]]
+        return remote(spot, spot, kh_s.at[row, half], kh_r.at[row, half], [right, left][half])
+
+    def relay_arrival(row, half):
+        spot = kv.at[[far_chip, far_across][row], c, halves[half]]
+        return remote(spot, spot, kh_s.at[row, half], kh_r.at[row, half], right)
 
     def core_send(slot):
         return remote(kv.at[slot, c], kv.at[slot, c], kc_s.at[slot], kc_r.at[slot], dev(0, 0, 1))
 
     def core_arrival(slot):
         return remote(kv.at[slot, 1 - c], kv.at[slot, 1 - c], kc_s.at[slot], kc_r.at[slot], dev(0, 0, 1))
-
-    core_send(chip).start()
-    kv_send(0).start()
-    kv_send(1).start()
-    kv_send(2).start()
 
     own_w = yh * 2 + c
     far_w = (1 - yh) * 2 + c
     w_local = pltpu.make_async_copy(w_ref, wraw.at[own_w], wl_s.at[0])
-    w_across = remote(w_ref, wraw.at[own_w], w_s.at[0], w_r.at[0], dev(1, 0, 0))
-    w_core = remote(w_ref, wraw.at[own_w], w_s.at[1], w_r.at[1], dev(0, 0, 1))
-    w_pass = remote(wraw.at[far_w], wraw.at[far_w], w_s.at[2], w_r.at[2], dev(0, 0, 1))
+    w_core = remote(w_ref, wraw.at[own_w], w_s.at[0], w_r.at[0], dev(0, 0, 1))
+
+    def w_across(half):
+        return remote(w_ref.at[halves[half]], wraw.at[own_w, halves[half]], w_s.at[1 + half], w_r.at[1 + half], dev(1, 0, 0))
+
+    def w_pass(half):
+        spot = wraw.at[far_w, halves[half]]
+        return remote(spot, spot, w_s.at[3 + half], w_r.at[3 + half], dev(0, 0, 1))
+
     w_local.start()
 
     for j in range(CH):
@@ -140,13 +149,20 @@
         m[j] = new
         acc[j] = acc[j] * jnp.exp2(old - new) + dg(values, p, 1, 0)
 
-    def sweep(keys, values, sections_of):
-        ahead = scores(keys, 0)
-        for j in range(CH):
+    def run(items):
+        ahead = None
+        for n, (before, keys, values, sections, j) in enumerate(items):
+            if n == 0:
+                before()
+                ahead = scores(keys(), j)
             s = ahead
-            if j + 1 < CH:
-                ahead = scores(keys, j + 1)
-            soften(j, s, values, sections_of(j))
+            if n + 1 < len(items):
+                items[n + 1][0]()
+                ahead = scores(items[n + 1][1](), items[n + 1][4])
+            soften(j, s, values(), sections())
+
+    def nothing():
+        return None
 
     my_turn = turn_ref[b]
 
@@ -169,53 +185,23 @@
             out.append((cc * 512 + 256, 256, later, None if limits is None else limits[cc]))
         return out
 
-    sweep(pre_ref[0], with_ones([pvt[i] for i in range(PREFIX // 128)]), lambda j: [(0, PREFIX, None, None)])
-
-    kv_send(3).start()
-    kv_arrival(across).wait_recv()
-    kv_forward(0).start()
-    kv_forward(1).start()
-    core_send(across).start()
+    def prefix_values():
+        return with_ones([pvt[i] for i in range(PREFIX // 128)])
+
+    run([(nothing, lambda: pre_ref[0], prefix_values, lambda: [(0, PREFIX, None, None)], j) for j in range(CH)])
+
+    pl.semaphore_wait(barrier, len(peers))
+    core_send(chip).start()
+    kv_send(0).start()
+    kv_send(1).start()
+    kv_send(2).start()
     w_core.start()
-    w_across.start()
     core_arrival(chip).wait_recv()
 
     def own_sections(j):
         position = lax.rem(lax.broadcasted_iota(jnp.int32, (1, QT), 1), ROWS) + j * ROWS
         limits = [position + jnp.where(chip * 2 + cc == b, 0, MSG) for cc in range(2)]
         return chip_sections(chip, limits)
-
-    sweep(chip_keys(chip), chip_values(chip), own_sections)
-    kv_forward(2).start()
-
-    order = [(0, 1), (0, 3), (1, 0), (0, 2), (1, 1), (1, 3), (1, 2)]
-    FIRST = len(order) - LAST
-
-    def slot_of(s):
-        return chip_at(pick(s, [p[0] for p in order]), pick(s, [p[1] for p in order]))
-
-    def fetch(s):
-        @pl.when(s != 2)
-        def _():
-            slot = slot_of(s)
-            kv_arrival(slot).wait_recv()
-            core_send(slot).start()
-
-    fetch(jnp.int32(0))
-
-    def first_part(s, carry):
-        slot = slot_of(s)
-        fetch(s + 1)
-        core_arrival(slot).wait_recv()
-        sweep(chip_keys(slot), chip_values(slot), lambda j: chip_sections(slot))
-        return carry
-
-    lax.fori_loop(0, FIRST, first_part, 0)
-
-    for s in range(FIRST + 1, len(order)):
-        fetch(jnp.int32(s))
-    for s in range(FIRST, len(order)):
-        core_arrival(slot_of(jnp.int32(s))).wait_recv()
 
     def arrange(y):
         def some_rows(i, carry):
@@ -228,37 +214,53 @@
             return carry
         lax.fori_loop(0, 8, some_rows, 0)
 
+    def chip_items(slot, sections, before=nothing):
+        return [(before if j == 0 else nothing, lambda: chip_keys(slot), lambda: chip_values(slot), lambda j=j: sections(j), j)
+                for j in range(CH)]
+
+    run(chip_items(chip, own_sections))
     w_local.wait()
     w_core.wait_recv()
     arrange(yh)
 
+    kv_arrival(right_chip).wait_recv()
+    kv_relay(0, 1).start()
+    core_send(right_chip).start()
+    kv_arrival(left_chip).wait_recv()
+    kv_relay(0, 0).start()
+    core_send(left_chip).start()
+    kv_arrival(across).wait_recv()
+    kv_forward(0).start()
+    kv_forward(1).start()
+    core_send(across).start()
+    for half in range(2):
+        w_across(half).start()
+    core_arrival(right_chip).wait_recv()
+
+    def before_left():
+        for half in range(2):
+            relay_arrival(0, half).wait_recv()
+        core_send(far_chip).start()
+        core_arrival(left_chip).wait_recv()
+
+    def before_across():
+        core_arrival(across).wait_recv()
+        kv_arrival(right_across).wait_recv()
+        kv_relay(1, 1).start()
+        core_send(right_across).start()
+        kv_arrival(left_across).wait_recv()
+        kv_relay(1, 0).start()
+        core_send(left_across).start()
+
+    run(chip_items(right_chip, lambda j: chip_sections(right_chip))
+        + chip_items(left_chip, lambda j: chip_sections(left_chip), before_left)
+        + chip_items(across, lambda j: chip_sections(across), before_across))
+
+    for slot in (far_chip, right_across, left_across):
+        core_arrival(slot).wait_recv()
+
     def a_send(j, r):
         return remote(ag.at[j, x], ag.at[j, x], a_s.at[j, r - 1], a_r.at[j, r - 1], dev(0, r, 0))
-
-    last_slots = [slot_of(jnp.int32(s)) for s in range(FIRST, len(order))]
-
-    def second_part(j, carry):
-        ahead = scores(chip_keys(last_slots[0]), j)
-        for n in range(LAST):
-            s = ahead
-            if n + 1 < LAST:
-                ahead = scores(chip_keys(last_slots[n + 1]), j)
-            soften(j, s, chip_values(last_slots[n]), chip_sections(last_slots[n]))
-        done = acc[j]
-        heads = (done[:HD] / done[HD:HD + 1]).T.astype(BF)
-        for h in range(HEADS):
-            ag[j, x, :, h * HD:(h + 1) * HD] = heads[h * ROWS:(h + 1) * ROWS, :]
-        for r in (1, 3, 2):
-            a_send(j, r).start()
-
-        @pl.when(j == CH - 2)
-        def _():
-            w_across.wait_recv()
-            w_pass.start()
-
-        return carry
-
-    lax.fori_loop(0, CH, second_part, 0)
 
     def ring_copy(st, s, d):
         to = dev(0, 0, 0, 1 if d == 0 else TR - 1)
@@ -289,7 +291,8 @@
 
         @pl.when(st == 1)
         def _():
-            w_pass.wait_recv()
+            w_pass(0).wait_recv()
+            w_pass(1).wait_recv()
             arrange(1 - yh)
 
         left = ag[j].reshape(4 * ROWS, HEADS * HD)
@@ -320,7 +323,7 @@
 
     def tick(T, carry):
         def one(st, inner):
-            s = T - st
+            s = T - pick(st, START)
 
             @pl.when(s == 0)
             def _():
@@ -338,7 +341,51 @@
 
         return lax.fori_loop(0, ST, one, carry)
 
-    lax.fori_loop(0, ST + TR - 1, tick, 0)
+    def before_second(j):
+        @pl.when(j == 0)
+        def _():
+            for half in range(2):
+                relay_arrival(1, half).wait_recv()
+            core_send(far_across).start()
+
+        @pl.when(j == CH - 1)
+        def _():
+            tick(0, 0)
+
+    def before_third(j):
+        return None
+
+    def before_last(j):
+        @pl.when(j == 0)
+        def _():
+            core_arrival(far_across).wait_recv()
+
+        @pl.when(j == CH - 1)
+        def _():
+            tick(1, 0)
+
+    def second_part(j, carry):
+        def item(slot, before):
+            return (lambda: before(j), lambda: chip_keys(slot), lambda: chip_values(slot), lambda: chip_sections(slot), j)
+
+        run([item(far_chip, lambda j: None), item(left_across, before_second), item(right_across, before_third),
+             item(far_across, before_last)])
+        done = acc[j]
+        heads = (done[:HD] / done[HD:HD + 1]).T.astype(BF)
+        for h in range(HEADS):
+            ag[j, x, :, h * HD:(h + 1) * HD] = heads[h * ROWS:(h + 1) * ROWS, :]
+        for r in (1, 3, 2):
+            a_send(j, r).start()
+        for half in range(2):
+            @pl.when(j == 1 + half)
+            def _():
+                w_across(half).wait_recv()
+                w_pass(half).start()
+
+        return carry
+
+    lax.fori_loop(0, CH, second_part, 0)
+    lax.fori_loop(2, START[-1] + TR, tick, 0)
 
     def drain(st, carry):
         for r in (1, 2, 3):
@@ -361,19 +408,21 @@
         return carry
 
     lax.fori_loop(0, CH, drain_heads, 0)
-    for i in range(4):
+    for i in range(3):
         kv_send(i).wait_send()
-    for i in range(3):
+    for i in range(2):
         kv_forward(i).wait_send()
+        w_across(i).wait_send()
+        w_pass(i).wait_send()
+        for row in range(2):
+            kv_relay(row, i).wait_send()
 
     def drain_core(slot, carry):
         core_send(slot).wait_send()
         return carry
 
     lax.fori_loop(0, 8, drain_core, 0)
-    w_across.wait_send()
     w_core.wait_send()
-    w_pass.wait_send()
 
 
 def per_device(queries, prefix_cache, prior_cache, fresh_cache, visible, turn_order, output_weight):
@@ -399,8 +448,8 @@
             pltpu.VMEM((ST, TR - 1, 2, 2 * ROWS, 128), BF),
             pltpu.VMEM((ST, TR - 1, 2, 2 * ROWS, 128), BF),
             pltpu.VMEM((ST, 4, ROWS, 128), BF),
-            dma((4,)), dma((8,)), dma((3,)), dma((8,)), dma((8,)),
-            dma((3,)), dma((3,)), dma((1,)),
+            dma((3,)), dma((8,)), dma((2,)), dma((2, 2)), dma((2, 2)), dma((8,)), dma((8,)),
+            dma((5,)), dma((5,)), dma((1,)),
             dma((CH, 3)), dma((CH, 3)),
             dma((ST, TR - 1, 2)), dma((ST, TR - 1, 2)),
             dma((ST, 3)), dma((ST, 3)),

time: 121 us -> 107 us (0.88)
  Pallas kernels: 119 us -> 105 us
    pallas_call x1, Pallas kernels: 119 us -> 105 us  [per_device(): pl.pallas_call(kernel, name='debate', out_shape=jax.ShapeDtypeStruct(quer...]
where the time goes in v2:
time: 107 us
  Pallas kernels  105 us (98%)
  local copies, waits for them, and re-layouts  1.87 us (2%)
    pallas_call x1, Pallas kernels, per_device(): pl.pallas_call(kernel, name='debate', out_shape=jax.ShapeDtypeStruct(quer...  105 us

profile of v2, /device:TPU:16, one launch (start us, length us, event | category | flops | bytes accessed | tf_op | source)
XLA Modules:
  0.0 106.8 jit_solution(15889748955044358697)
XLA Ops:
  0.0 104.9 %debate.1 = bf16[256,1024]{1,0:T(8,128)(2,1)} custom-call(bf16[256,1024]{1,0:T(8,128)(2,1)} %q_ref.1, bf16[2,1536,128]{2,1,0:T(8,128)(2,1)} %pre_ref.1, bf16[2,256,128]{2,1,0:T(8,128)(2,1)} %pri_ref.1, bf16[2,256,128]{2,1,0:T(8,128)(2,1)} %fre_ref.1, s32[16,16]{1,0:T(8,128)} %vis_ref.1, s32[16]{0:T(128)} %turn_ref.1, bf16[1024,512]{1,0:T(8,128)(2,1)} %w_ref.1), custom_call_target="tpu_custom_call" | custom-call | flops 15000000512 | bytes 6000000 | tf_op jit(solution)/shard_map/debate/pallas_call | solution.py:432
  105.0 1.9 %copy.9 = bf16[256,1024]{1,0:T(8,128)(2,1)} copy(bf16[256,1024]{1,0:T(8,128)(2,1)} %debate.1) | data formatting | bytes 1048576

commit v3 on v2

--- a/solution.py
+++ b/solution.py
@@ -17,7 +17,7 @@
 QT = ROWS * HEADS
 TR = 8
 ST = 2 * CH
-START = (0, 1, 2, 2, 2, 3, 3, 3)
+START = (0, 1, 2, 2, 2, 2, 3, 3)
 SCALE = math.log2(math.e) / math.sqrt(HD)
 BIG = 1e30
 BF = jnp.bfloat16

time: 107 us -> 107 us (level)
  no operation moved by 1% of the time
where the time goes in v3:
time: 107 us
  Pallas kernels  105 us (98%)
  local copies, waits for them, and re-layouts  1.87 us (2%)
    pallas_call x1, Pallas kernels, per_device(): pl.pallas_call(kernel, name='debate', out_shape=jax.ShapeDtypeStruct(quer...  105 us

profile of v3, /device:TPU:16, one launch (start us, length us, event | category | flops | bytes accessed | tf_op | source)
XLA Modules:
  0.0 106.8 jit_solution(17774965803377679129)
XLA Ops:
  0.0 105.0 %debate.1 = bf16[256,1024]{1,0:T(8,128)(2,1)} custom-call(bf16[256,1024]{1,0:T(8,128)(2,1)} %q_ref.1, bf16[2,1536,128]{2,1,0:T(8,128)(2,1)} %pre_ref.1, bf16[2,256,128]{2,1,0:T(8,128)(2,1)} %pri_ref.1, bf16[2,256,128]{2,1,0:T(8,128)(2,1)} %fre_ref.1, s32[16,16]{1,0:T(8,128)} %vis_ref.1, s32[16]{0:T(128)} %turn_ref.1, bf16[1024,512]{1,0:T(8,128)(2,1)} %w_ref.1), custom_call_target="tpu_custom_call" | custom-call | flops 15000000512 | bytes 6000000 | tf_op jit(solution)/shard_map/debate/pallas_call | solution.py:432
  105.0 1.9 %copy.9 = bf16[256,1024]{1,0:T(8,128)(2,1)} copy(bf16[256,1024]{1,0:T(8,128)(2,1)} %debate.1) | data formatting | bytes 1048576

commit v4 on v2

--- a/solution.py
+++ b/solution.py
@@ -219,29 +219,30 @@
                 for j in range(CH)]
 
     run(chip_items(chip, own_sections))
+    kv_arrival(across).wait_recv()
+    kv_forward(0).start()
+    kv_forward(1).start()
+    kv_arrival(right_chip).wait_recv()
+    core_send(right_chip).start()
+    kv_arrival(left_chip).wait_recv()
+    core_send(left_chip).start()
+    core_send(across).start()
+    for half in range(2):
+        w_across(half).start()
     w_local.wait()
     w_core.wait_recv()
     arrange(yh)
-
-    kv_arrival(right_chip).wait_recv()
-    kv_relay(0, 1).start()
-    core_send(right_chip).start()
-    kv_arrival(left_chip).wait_recv()
-    kv_relay(0, 0).start()
-    core_send(left_chip).start()
-    kv_arrival(across).wait_recv()
-    kv_forward(0).start()
-    kv_forward(1).start()
-    core_send(across).start()
-    for half in range(2):
-        w_across(half).start()
     core_arrival(right_chip).wait_recv()
 
     def before_left():
+        for half in range(2):
+            kv_relay(0, half).start()
+        core_arrival(left_chip).wait_recv()
+
+    def far_arrives():
         for half in range(2):
             relay_arrival(0, half).wait_recv()
         core_send(far_chip).start()
-        core_arrival(left_chip).wait_recv()
 
     def before_across():
         core_arrival(across).wait_recv()
@@ -252,11 +253,13 @@
         kv_relay(1, 0).start()
         core_send(left_across).start()
 
+    across_items = chip_items(across, lambda j: chip_sections(across), before_across)
+    across_items[2] = (far_arrives,) + across_items[2][1:]
     run(chip_items(right_chip, lambda j: chip_sections(right_chip))
         + chip_items(left_chip, lambda j: chip_sections(left_chip), before_left)
-        + chip_items(across, lambda j: chip_sections(across), before_across))
-
-    for slot in (far_chip, right_across, left_across):
+        + across_items)
+
+    for slot in (right_across, left_across):
         core_arrival(slot).wait_recv()
 
     def a_send(j, r):
@@ -353,7 +356,9 @@
             tick(0, 0)
 
     def before_third(j):
-        return None
+        @pl.when(j == 0)
+        def _():
+            core_arrival(far_chip).wait_recv()
 
     def before_last(j):
         @pl.when(j == 0)
@@ -368,7 +373,7 @@
         def item(slot, before):
             return (lambda: before(j), lambda: chip_keys(slot), lambda: chip_values(slot), lambda: chip_sections(slot), j)
 
-        run([item(far_chip, lambda j: None), item(left_across, before_second), item(right_across, before_third),
+        run([item(left_across, lambda j: None), item(right_across, before_second), item(far_chip, before_third),
              item(far_across, before_last)])
         done = acc[j]
         heads = (done[:HD] / done[HD:HD + 1]).T.astype(BF)

time: 107 us -> 106 us (level)
  Pallas kernels: 105 us -> 103 us
    pallas_call x1, Pallas kernels: 105 us -> 103 us  [per_device(): pl.pallas_call(kernel, name='debate', out_shape=jax.ShapeDtypeStruct(quer...]
where the time goes in v4:
time: 106 us; the launch traced here: 105 us
  Pallas kernels  103 us (97%)
  local copies, waits for them, and re-layouts  1.87 us (2%)
    pallas_call x1, Pallas kernels, per_device(): pl.pallas_call(kernel, name='debate', out_shape=jax.ShapeDtypeStruct(quer...  103 us

profile of v4, /device:TPU:16, one launch (start us, length us, event | category | flops | bytes accessed | tf_op | source)
XLA Modules:
  0.0 105.1 jit_solution(2664233990614940083)
XLA Ops:
  0.0 103.2 %debate.1 = bf16[256,1024]{1,0:T(8,128)(2,1)} custom-call(bf16[256,1024]{1,0:T(8,128)(2,1)} %q_ref.1, bf16[2,1536,128]{2,1,0:T(8,128)(2,1)} %pre_ref.1, bf16[2,256,128]{2,1,0:T(8,128)(2,1)} %pri_ref.1, bf16[2,256,128]{2,1,0:T(8,128)(2,1)} %fre_ref.1, s32[16,16]{1,0:T(8,128)} %vis_ref.1, s32[16]{0:T(128)} %turn_ref.1, bf16[1024,512]{1,0:T(8,128)(2,1)} %w_ref.1), custom_call_target="tpu_custom_call" | custom-call | flops 15000000512 | bytes 6000000 | tf_op jit(solution)/shard_map/debate/pallas_call | solution.py:437
  103.2 1.9 %copy.9 = bf16[256,1024]{1,0:T(8,128)(2,1)} copy(bf16[256,1024]{1,0:T(8,128)(2,1)} %debate.1) | data formatting | bytes 1048576
